TPU v7x, 32 devices: a whole 2x2x4 slice. The times are simulated.
32 devices in a mesh: seq: 8 (over z, x), shard: 4 (over y, core).
Axes of the slice: x: 2, y: 2, z: 4, core: 2. Of those that a mesh axis runs over, the one named last changes fastest.
Arguments:
- tokens: bfloat16 [4, 1920, 1536], P('shard', 'seq'), may hold values from -6 to 6
- gains_taps: float32 [5, 1536], replicated, may hold values from 0.5 to 1.5
- weights: float32 [1536, 26880], P('seq', 'shard'), may hold values from -0.15625 to 0.15625
- cotangent: bfloat16 [4, 1920, 1536], P('shard', 'seq'), may hold values from -6 to 6
- weight_first: float32 [1536, 26880], P('seq', 'shard'), may hold values from -56 to 56
- weight_second: float32 [1536, 26880], P('seq', 'shard'), may hold values from 76.8 to 3840
- gains_first: float32 [5, 1536], replicated, may hold values from -56 to 56
- gains_second: float32 [5, 1536], replicated, may hold values from 76.8 to 3840
Outputs:
- block_out: bfloat16 [4, 1920, 1536], P('shard', 'seq')
- input_grad: bfloat16 [4, 1920, 1536], P('shard', 'seq')
- weight_grad: float32 [1536, 26880], P('seq', 'shard')
- weight_first_new: float32 [1536, 26880], P('seq', 'shard')
- weight_second_new: float32 [1536, 26880], P('seq', 'shard')
- weight_new: float32 [1536, 26880], P('seq', 'shard')
- gains_grad: float32 [5, 1536], replicated
- gains_first_new: float32 [5, 1536], replicated
- gains_second_new: float32 [5, 1536], replicated
- gains_new: float32 [5, 1536], replicated
All inputs are finite; a program needn't handle non-finite values.
Results may differ from a plain program's by a relative error of at most 0.012.
The roundings to bfloat16 on the way count: a program that leaves them out, or rounds other values in their place, can miss the bound.
Values may be sent and summed in bfloat16 or wider, within the bound.
A program may use at most 640 MiB of HBM per device.

v0:
```python
import functools

import jax
import jax.numpy as jnp
from jax import lax
from jax.experimental import pallas as pl
from jax.experimental.pallas import tpu as pltpu
from jax.sharding import PartitionSpec as P

D = 1536
FF = 6912
STEP = 10
GROUPS = 4
QUARTER = D // GROUPS
UNITS = FF // GROUPS
GROUP_COLS = 4 * QUARTER + 3 * UNITS
HALF_Q = QUARTER // 2
HALF_F = UNITS // 2
LANES = 128
PAD_F = -(-HALF_F // LANES) * LANES
WIDE = 256
CONV_COLS = 4 * HALF_Q
UNIT_CHUNKS = (384, 256, PAD_F - 640)
UNIT_STARTS = (0, 384, 640)
WIDTHS = (CONV_COLS,) + tuple(3 * units for units in UNIT_CHUNKS)
STARTS = tuple(sum(WIDTHS[:k]) for k in range(len(WIDTHS)))
SPREAD_SPLITS = (208, 208, 64, 128)
COLLECT_SPLITS = (128, 128, 112, 112)
REACH = (1, 1, 1, 1)
CUT_FIRST = 1
SLICE = 384
TILE = 16
ROWS = 48

MOMENT_DECAY = 0.9
SQUARE_DECAY = 0.95
ADAM_EPSILON = 1e-08
NORM_EPSILON = 1e-05
WEIGHT_RATE = 0.02
GAIN_RATE = 0.2
WEIGHT_DECAY = 0.1

BF16 = jnp.bfloat16
F32 = jnp.float32
MESH = pl.DeviceIdType.MESH
VMEM_BYTES = 63 * 1024 * 1024


def place():
    seq, shard = lax.axis_index("seq"), lax.axis_index("shard")
    inner, core = lax.rem(seq, 2), lax.rem(shard, 2)
    return seq, shard, inner, core


def partners():
    seq, shard, inner, core = place()
    across = {"seq": seq + 1 - 2 * inner, "shard": shard}
    beside = {"seq": seq, "shard": lax.rem(shard + 2, 4)}
    twin = {"seq": seq, "shard": shard + 1 - 2 * core}
    return across, beside, twin


def remote(src, dst, send, recv, device):
    return pltpu.make_async_remote_copy(
        src_ref=src, dst_ref=dst, send_sem=send, recv_sem=recv, device_id=device, device_id_type=MESH
    )


def line():
    seq, shard, _, _ = place()
    size = lax.axis_size("seq")
    return seq // 2, lambda steps: {"seq": lax.rem(seq + 2 * steps + size, size), "shard": shard}


def greet(layers):
    outer, at = line()
    barrier = pltpu.get_barrier_semaphore()
    for device in partners():
        pl.semaphore_signal(barrier, inc=1, device_id=device, device_id_type=MESH)
    for steps in range(1, layers):
        for sign in (1, -1):

            @pl.when(in_line(outer + sign * steps, layers))
            def _():
                pl.semaphore_signal(barrier, inc=1, device_id=at(sign * steps), device_id_type=MESH)


def greeted(layers):
    pl.semaphore_wait(pltpu.get_barrier_semaphore(), 3 + layers - 1)


def in_line(index, layers):
    return (index >= 0) & (index < layers)


def allow(credit):
    for device in partners():
        pl.semaphore_signal(credit, inc=1, device_id=device, device_id_type=MESH)


def dot(left, right):
    return jnp.dot(left, right, preferred_element_type=F32)


def dot_rows(left, right):
    return lax.dot_general(left, right, (((1,), (1,)), ((), ())), preferred_element_type=F32)


def dot_columns(left, right):
    return lax.dot_general(left, right, (((0,), (0,)), ((), ())), preferred_element_type=F32)


def aligned(start, size, multiple=16):
    return pl.ds(pl.multiple_of(start, multiple), size)


class Gather:
    def __init__(self, layers, rows, oth, outs, send_x, recv_x, send_z, recv_z):
        self.layers, self.rows, self.oth, self.outs = layers, rows, oth, outs
        self.send_x, self.recv_x, self.send_z, self.recv_z = send_x, recv_x, send_z, recv_z
        self.seq, _, self.inner, _ = place()
        self.outer, self.at = line()
        self.across = partners()[0]

    def seq_rows(self, index):
        return aligned(index * self.rows, self.rows)

    def layer_rows(self, direction, distance):
        origin = self.outer - distance if direction == 0 else self.outer + distance
        return aligned(origin * 2 * self.rows, 2 * self.rows)

    def copy(self, k, src, dst, direction, distance, hop, piece):
        slot = (k, direction, distance + hop - 1, piece)
        return remote(
            src, dst, self.send_z.at[slot], self.recv_z.at[slot], self.at(hop if direction == 0 else -hop)
        )

    def goes(self, direction, hop):
        return in_line(self.outer + (hop if direction == 0 else -hop), self.layers)

    def has_come(self, direction, distance):
        return in_line(self.outer + (-distance if direction == 0 else distance), self.layers)

    def hops(self, k, distance):
        return range(1, min(REACH[k], self.layers - 1 - distance) + 1)

    def own_copy(self, k, direction, hop):
        here = self.outs[k].at[self.seq_rows(self.seq)]
        return self.copy(k, here, here, direction, 0, hop, 0)

    def other_copy(self, k, direction, hop):
        there = self.outs[k].at[self.seq_rows(self.seq + 1 - 2 * self.inner)]
        return self.copy(k, there, there, direction, 0, hop, 1)

    def pass_copy(self, k, direction, distance, hop):
        ref = self.outs[k].at[self.layer_rows(direction, distance)]
        return self.copy(k, ref, ref, direction, distance, hop, 0)

    def other_rows(self, k):
        return self.oth.at[pl.ds(k * self.rows, self.rows), pl.ds(0, WIDTHS[k])]

    def exchange(self, k):
        self.x_copy(k).start()

    def x_copy(self, k):
        here = self.outs[k].at[self.seq_rows(self.seq)]
        return remote(self.other_rows(k), here, self.send_x.at[k], self.recv_x.at[k], self.across)

    def crossed(self):
        for k in range(len(self.outs)):
            self.x_copy(k).wait_send()

    def send_own(self, k):
        for hop in self.hops(k, 0):
            for direction in (0, 1):

                @pl.when(self.goes(direction, hop))
                def _():
                    self.own_copy(k, direction, hop).start()

    def send_other(self, k):
        self.x_copy(k).wait_recv()
        for hop in self.hops(k, 0):
            for direction in (0, 1):

                @pl.when(self.goes(direction, hop))
                def _():
                    self.other_copy(k, direction, hop).start()

    def step(self, k, distance):
        for direction in (0, 1):

            @pl.when(self.has_come(direction, distance))
            def _():
                if distance <= REACH[k]:
                    origin = self.outer - distance if direction == 0 else self.outer + distance
                    for piece in (0, 1):
                        index = 2 * origin + (self.inner if piece == 0 else 1 - self.inner)
                        ref = self.outs[k].at[self.seq_rows(index)]
                        self.copy(k, ref, ref, direction, distance - 1, 1, piece).wait_recv()
                else:
                    ref = self.outs[k].at[self.layer_rows(direction, distance)]
                    self.copy(k, ref, ref, direction, distance - 1, 1, 0).wait_recv()
                if distance % REACH[k] == 0:
                    for hop in self.hops(k, distance):

                        @pl.when(self.goes(direction, hop))
                        def _():
                            self.pass_copy(k, direction, distance, hop).start()

    def steps(self, k, first, last=None):
        last = self.layers - 1 if last is None else min(last, self.layers - 1)
        for distance in range(first, last + 1):
            self.step(k, distance)

    def finish(self):
        for k in range(len(self.outs)):
            for distance in range(0, self.layers - 1, REACH[k]):
                for hop in self.hops(k, distance):
                    for direction in (0, 1):

                        @pl.when(self.goes(direction, hop) & self.has_come(direction, distance))
                        def _():
                            if distance == 0:
                                self.own_copy(k, direction, hop).wait_send()
                                self.other_copy(k, direction, hop).wait_send()
                            else:
                                self.pass_copy(k, direction, distance, hop).wait_send()


class Reduce:
    def __init__(self, layers, rows, grads, slots, stage, spare, total, outgoing, mine, theirs, sems):
        self.layers, self.rows, self.grads, self.slots = layers, rows, grads, slots
        self.stage, self.spare, self.total, self.outgoing = stage, spare, total, outgoing
        self.mine, self.theirs = mine, theirs
        self.send_g, self.recv_g, self.fetched, self.fetches, self.stored, self.send_o, self.recv_o = sems
        _, _, self.inner, _ = place()
        self.outer, self.at = line()
        self.across = partners()[0]

    def owner(self, direction, distance):
        return self.outer + distance if direction == 0 else self.outer - distance

    def upstream(self, direction, steps):
        return in_line(self.outer - steps if direction == 0 else self.outer + steps, self.layers)

    def block(self, k, owner):
        return self.grads[k].at[aligned(owner * 2 * self.rows, 2 * self.rows), pl.ds(0, WIDTHS[k])]

    def copy(self, k, src, direction, distance):
        slot = (direction, distance - 1)
        return remote(
            src,
            self.slots[k].at[slot],
            self.send_g.at[(k,) + slot],
            self.recv_g.at[(k,) + slot],
            self.at(1 if direction == 0 else -1),
        )

    def send(self, k, direction, distance):
        self.copy(k, self.block(k, self.owner(direction, distance)), direction, distance).start()

    def direct(self, k, part=None, least=1, most=None):
        for distance in range(most or self.layers - 1, least - 1, -1):
            for direction in (0, 1):
                owner = self.owner(direction, distance)
                here = in_line(owner, self.layers) & jnp.logical_not(self.upstream(direction, 1))
                if part is not None:
                    here = here & (owner * 2 * self.rows // SLICE == part)

                @pl.when(here)
                def _():
                    self.send(k, direction, distance)

    def fetch(self, k, direction, distance):
        slot = self.slots[k].at[direction, distance - 1]
        self.copy(k, slot, direction, distance).wait_recv()
        held = self.stage.at[:, pl.ds(0, WIDTHS[k])]
        copy = pltpu.make_async_copy(slot, held, self.fetched)
        copy.start()
        copy.wait()

    def tiles(self, body):
        def step(n, _):
            body(aligned(n * TILE, TILE))
            return 0

        lax.fori_loop(0, 2 * self.rows // TILE, step, 0)

    def join(self, k, most, least):
        cols = pl.ds(0, WIDTHS[k])
        for distance in range(most, least - 1, -1):
            for direction in (0, 1):
                owner = self.owner(direction, distance)

                @pl.when(in_line(owner, self.layers) & self.upstream(direction, 1))
                def _():
                    def add(tile):
                        base = self.owner(direction, distance) * 2 * self.rows
                        rows = pl.ds(pl.multiple_of(base + tile.start, 16), TILE)
                        ref = self.grads[k]
                        ref[rows, cols] = (
                            ref[rows, cols].astype(F32) + self.stage[tile, cols].astype(F32)
                        ).astype(BF16)

                    self.fetch(k, direction, distance + 1)
                    self.tiles(add)
                    self.send(k, direction, distance)

    def final(self, k, before=None):
        cols = pl.ds(0, WIDTHS[k])
        came = [(1, 0), (1, 1)]

        def fetch(n, distance, direction):
            return pltpu.make_async_copy(
                self.slots[k].at[direction, distance - 1],
                self.spare.at[pl.ds(n * 2 * self.rows, 2 * self.rows), cols],
                self.fetches.at[n],
            )

        for n, (distance, direction) in enumerate(came):

            @pl.when(self.upstream(direction, distance))
            def _():
                self.copy(k, self.slots[k].at[direction, distance - 1], direction, distance).wait_recv()
                fetch(n, distance, direction).start()

        if before is not None:
            self.store(before).wait()

        here, there = self.inner * self.rows, (1 - self.inner) * self.rows

        def each(base, body):
            def step(n, _):
                body(base + n * TILE, n * TILE)
                return 0

            lax.fori_loop(0, self.rows // TILE, step, 0)

        for n, (distance, direction) in enumerate(came):

            @pl.when(self.upstream(direction, distance))
            def _():
                fetch(n, distance, direction).wait()

        def add_up(flags):
            def total(rows):
                value = self.grads[k][aligned(self.outer * 2 * self.rows + rows, TILE), cols].astype(F32)
                for n, flag in enumerate(flags):
                    if flag:
                        value = value + self.spare[aligned(n * 2 * self.rows + rows, TILE), cols].astype(F32)
                return value

            def send(rows, at):
                self.outgoing[aligned(at, TILE), pl.ds(STARTS[k], WIDTHS[k])] = total(rows).astype(BF16)

            def keep(rows, at):
                self.total[aligned(at, TILE), cols] = total(rows)

            each(there, send)
            self.over(k).start()
            each(here, keep)
            self.store(k).start()

        patterns = {}
        for place_in_line in range(self.layers):
            flags = tuple(
                0 <= (place_in_line - distance if direction == 0 else place_in_line + distance) < self.layers
                for distance, direction in came
            )
            patterns.setdefault(flags, []).append(place_in_line)
        for flags, places in patterns.items():
            here_now = functools.reduce(jnp.logical_or, [self.outer == p for p in places])

            @pl.when(here_now)
            def _():
                add_up(flags)

    def over(self, k):
        wide = pl.ds(STARTS[k], WIDTHS[k])
        return remote(
            self.outgoing.at[:, wide], self.theirs.at[:, wide], self.send_o.at[k], self.recv_o.at[k], self.across
        )

    def store(self, k):
        return pltpu.make_async_copy(
            self.total.at[:, pl.ds(0, WIDTHS[k])], self.mine.at[:, pl.ds(STARTS[k], WIDTHS[k])], self.stored.at[k]
        )

    def wait_sent(self, k):
        for distance in range(1, self.layers):
            for direction in (0, 1):
                owner = self.owner(direction, distance)

                @pl.when(in_line(owner, self.layers))
                def _():
                    self.copy(k, self.block(k, owner), direction, distance).wait_send()

    def finish(self, before):
        self.store(before).wait()
        for k in range(len(self.grads)):
            self.over(k).wait()


class Spread:
    slots = range(11)

    def __init__(self, buf, seg, split, send, recv):
        self.buf, self.seg, self.split, self.send, self.recv = buf, seg, split, send, recv

    def index(self, n):
        _, shard, inner, core = place()
        row, flip, other = (n // 2) % 2, n // 4, n % 2
        return 2 * (lax.rem(shard + 2 * row, 4) + other * (1 - 2 * core)) + inner + flip * (1 - 2 * inner)

    def copy(self, slot):
        across, beside, twin = partners()
        low, high, whole = (0, self.split), (self.split, self.seg - self.split), (0, self.seg)
        n, (first, size), device = {
            0: (0, low, across),
            9: (0, high, across),
            1: (0, high, beside),
            10: (0, low, beside),
            2: (0, whole, twin),
            3: (4, low, beside),
            4: (4, whole, twin),
            5: (2, high, across),
            6: (2, whole, twin),
            7: (6, low, twin),
            8: (6, high, twin),
        }[slot]
        ref = self.buf.at[aligned(self.index(n) * self.seg + first, size)]
        return remote(ref, ref, self.send.at[slot], self.recv.at[slot], device)

    def push(self, *slots):
        for slot in slots:
            self.copy(slot).start()

    def came(self, *slots):
        for slot in slots:
            self.copy(slot).wait_recv()

    def start(self):
        self.push(0, 1, 9, 10, 2)

    def first(self):
        self.came(1)
        self.push(5)
        self.came(0)
        self.push(3)

    def near(self):
        self.came(10)
        self.push(6)
        self.came(9)
        self.push(4)

    def far(self):
        self.came(3)
        self.push(7)
        self.came(5)
        self.push(8)

    def sent(self):
        for slot in self.slots:
            self.copy(slot).wait_send()

    def end(self):
        self.came(2, 4, 6, 7, 8)
        self.sent()

    def before(self, n):
        return {
            1: (lambda: self.came(2),),
            2: (self.first, self.near),
            3: (lambda: self.came(6),),
            5: (lambda: self.came(4),),
            6: (self.far,),
            7: (lambda: self.came(7, 8),),
        }.get(n, ())


class Collect:
    def __init__(self, part, seg, split, total, pair, near, joined, send, recv):
        self.part, self.seg, self.total = part, seg, total
        self.pair, self.near, self.joined, self.send, self.recv = pair, near, joined, send, recv
        _, self.shard, self.inner, core = place()
        self.twin_shard = self.shard + 1 - 2 * core
        self.low, self.high, self.whole = (0, split), (split, seg - split), (0, seg)
        self.cols = pl.ds(0, D)

    def index(self, s, k):
        row, flip = 1 - k % 2, 1 - k // 2
        return 2 * lax.rem(s + 2 * row, 4) + self.inner + flip * (1 - 2 * self.inner)

    def pair_copy(self, k):
        src = self.part.at[aligned(self.index(self.twin_shard, k) * self.seg, self.seg), self.cols]
        return remote(src, self.pair.at[k], self.send.at[k], self.recv.at[k], partners()[2])

    def copy(self, slot):
        across, beside, _ = partners()
        src, dst, (first, size), device = {
            4: (self.pair.at[0], self.joined, self.low, across),
            5: (self.pair.at[0], self.joined, self.high, beside),
            6: (self.pair.at[1], self.near.at[0], self.low, across),
            7: (self.pair.at[2], self.near.at[1], self.high, beside),
            8: (self.pair.at[2], self.near.at[1], self.low, beside),
            9: (self.pair.at[1], self.near.at[0], self.high, across),
        }[slot]
        rows = pl.ds(first, size)
        return remote(src.at[rows], dst.at[rows], self.send.at[slot], self.recv.at[slot], device)

    def over(self, span, body):
        def step(n, _):
            body(aligned(span[0] + n * 16, 16))
            return 0

        lax.fori_loop(0, span[1] // 16, step, 0)

    def mine(self, k, rows):
        return self.part[aligned(self.index(self.shard, k) * self.seg + rows.start, 16), self.cols].astype(F32)

    def add_pair(self, k):
        def add(rows):
            self.pair[k, rows] = (self.mine(k, rows) + self.pair[k, rows].astype(F32)).astype(BF16)

        self.pair_copy(k).wait_recv()
        self.over(self.whole, add)
        for slot in ((4, 5), (6,), (7,))[k]:
            self.copy(slot).start()

    def add_own(self):
        def add(rows):
            self.total[rows] = self.mine(3, rows) + self.pair[3, rows].astype(F32)

        self.pair_copy(3).wait_recv()
        self.over(self.whole, add)

    def pass_on(self):
        for slot, k, span, after in ((4, 2, self.low, 8), (5, 1, self.high, 9)):

            def add(rows):
                self.pair[k, rows] = (self.pair[k, rows].astype(F32) + self.joined[rows].astype(F32)).astype(BF16)

            self.copy(slot).wait_recv()
            self.over(span, add)
            self.copy(after).start()

    def push(self):
        for k in range(4):
            self.pair_copy(k).start()

    def make(self, n, produce):
        k, own = n // 2, n % 2
        produce(self.index(jnp.where(own == 1, self.shard, self.twin_shard), k))

        @pl.when(own == 0)
        def _():
            self.pair_copy(k).start()

        for m in range(3):

            @pl.when(n == 2 * m + 1)
            def _():
                self.add_pair(m)
                if m == 2:
                    self.pass_on()

        pl.when(n == 7)(self.add_own)

    def end(self):
        def add(rows):
            near = self.near[0, rows].astype(F32) + self.near[1, rows].astype(F32)
            self.total[rows] = self.total[rows] + near

        for slots, span in (((6, 8), self.low), ((7, 9), self.high)):
            for slot in slots:
                self.copy(slot).wait_recv()
            self.over(span, add)
        for k in range(4):
            self.pair_copy(k).wait_send()
        for slot in range(4, 10):
            self.copy(slot).wait_send()


def norm_scale(values):
    return lax.rsqrt(jnp.mean(values * values, axis=-1, keepdims=True) + NORM_EPSILON)


def by_rows(rows, body, carry=0):
    def step(n, carry):
        return body(aligned(n * ROWS, ROWS), carry)

    return lax.fori_loop(0, rows // ROWS, step, carry)


def norm_back(values, gain, upstream):
    scale = norm_scale(values)
    scaled = gain * upstream
    inner = jnp.mean(scaled * values, axis=-1, keepdims=True)
    return (
        scale * scaled - values * scale * scale * scale * inner,
        jnp.sum(upstream * values * scale, axis=0, keepdims=True),
    )


REFS = (
    "tok", "cot", "gains", "weights",
    "block_out", "input_grad", "gain_sums", "mine", "theirs", "n1_held", "slot0", "slot1", "slot2", "slot3",
    "w0", "w1", "w2", "w3", "seq_a", "seq_b", "du", "act", "c_all", "gated", "mixed", "resid", "dresid", "total",
    "pair", "near", "joined", "g1", "g2", "g3", "stage", "sum", "tail", "outgoing", "tap_sums", "gain_in", "gain_line",
    "held", "loaded", "send_x", "recv_x", "send_z", "recv_z", "send_s", "recv_s", "send_c", "recv_c", "credit",
    "halo_send", "halo_recv", "send_g", "recv_g", "fetched", "fetches", "stored", "send_o", "recv_o",
    "send_a", "recv_a", "send_l", "recv_l",
)


def column_pieces(half):
    pieces = [(m * QUARTER + half * HALF_Q, m * HALF_Q, HALF_Q, 0) for m in range(4)]
    for k, (start, units) in enumerate(zip(UNIT_STARTS, UNIT_CHUNKS), 1):
        real = min(units, HALF_F - start)
        for m in range(3):
            first = 4 * QUARTER + m * UNITS + half * HALF_F + start
            pieces.append((first, STARTS[k] + m * units, real, units - real))
    return pieces


def block_kernel(layers, rows, *all_refs):
    r = dict(zip(REFS, all_refs, strict=True))
    tok, cot, gains = r["tok"], r["cot"], r["gains"]
    seq_a, seq_b, du, act = r["seq_a"], r["seq_b"], r["du"], r["act"]
    c_all, gated, mixed, total = r["c_all"], r["gated"], r["mixed"], r["total"]
    weights = (r["w0"], r["w1"], r["w2"], r["w3"])
    seg = tok.shape[0]
    _, shard, inner, _ = place()
    outer, at = line()
    me = 2 * shard + inner
    my_rows = aligned(me * seg, seg)
    chunks = list(zip(range(1, 1 + len(UNIT_CHUNKS)), UNIT_STARTS, UNIT_CHUNKS))
    gather = Gather(
        layers, rows, r["g1"], weights, r["send_x"], r["recv_x"], r["send_z"], r["recv_z"]
    )
    reduce = Reduce(
        layers, rows, (r["w2"], r["g1"], r["g2"], r["g3"]), (r["slot0"], r["slot1"], r["slot2"], r["slot3"]),
        r["stage"], r["w1"], r["sum"], r["outgoing"], r["mine"], r["theirs"],
        (r["send_g"], r["recv_g"], r["fetched"], r["fetches"], r["stored"], r["send_o"], r["recv_o"]),
    )

    def spread(buf, n):
        return Spread(buf, seg, SPREAD_SPLITS[n], r["send_s"].at[n], r["recv_s"].at[n])

    def collect(part, n):
        sems = r["send_c"].at[n], r["recv_c"].at[n]
        return Collect(part, seg, COLLECT_SPLITS[n], total, r["pair"], r["near"], r["joined"], *sems)

    one, up, two, three = spread(seq_a, 0), spread(seq_b, 1), spread(seq_a, 2), spread(seq_a, 3)
    branch, down, feed, inputs = collect(seq_a, 0), collect(seq_b, 1), collect(du, 2), collect(seq_a, 3)
    lanes = lax.broadcasted_iota(jnp.int32, (seg, WIDE), 1) < HALF_Q
    taps = pltpu.roll(gains[...], lax.rem(D - shard * QUARTER - inner * HALF_Q, D), 1)[2:5, :WIDE]
    kept = pl.ds(D, WIDE)
    sums, tap_sums = r["gain_sums"], r["tap_sums"]

    def block(t):
        return aligned(t * seg, seg)

    def mine(part):
        return pl.ds(pl.multiple_of(me * seg + part.start, 16), part.size)

    def first_norm():
        def rows(part, _):
            values = tok[part].astype(F32)
            seq_a[mine(part)] = (values * norm_scale(values) * gains[0:1, :]).astype(BF16)
            return 0

        by_rows(seg, rows)

    def up_start():
        seq_b[my_rows] = cot[...]
        up.start()

    def held():
        return pltpu.make_async_copy(seq_a, r["n1_held"], r["held"])

    def reload():
        return pltpu.make_async_copy(r["n1_held"], seq_b, r["held"])

    def project(s):
        for i in (0, 1):
            parts = dot(seq_a[block(2 * s + i)], weights[0][...])
            b = jnp.where(lanes, parts[:, :WIDE], 0.0)
            c = pltpu.roll(parts[:, 128 : 128 + 384], 384 - 64, 1)[:, :WIDE]
            x = parts[:, 384 : 384 + WIDE]
            c_all[s, pl.ds(i * seg, seg)] = jnp.where(lanes, c, 0.0)
            gated[s, pl.ds(8 + i * seg, seg)] = (b * x).astype(BF16).astype(F32)

    def ahead():
        return remote(
            gated.at[:, pl.ds(2 * seg, 8)], gated.at[:, pl.ds(0, 8)], r["halo_send"].at[0], r["halo_recv"].at[0], at(1)
        )

    def halo():
        pl.when(outer < layers - 1)(lambda: ahead().start())

        @pl.when(outer == 0)
        def _():
            gated[:, pl.ds(0, 8)] = jnp.zeros((GROUPS, 8, WIDE), F32)

    def convolved(s, i):
        return (
            taps[0:1, :] * gated[s, pl.ds(6 + i * seg, seg)]
            + taps[1:2, :] * gated[s, pl.ds(7 + i * seg, seg)]
            + taps[2:3, :] * gated[s, pl.ds(8 + i * seg, seg)]
        )

    def convolve(t):
        for i in (0, 1):

            @pl.when(t % 2 == i)
            def _():
                s = t // 2
                mixed[block(t)] = pltpu.roll(c_all[s, pl.ds(i * seg, seg)] * convolved(s, i), 64, 1).astype(BF16)

        seq_a[block(t)] = dot_rows(mixed[block(t)], weights[0][:, pl.ds(512, WIDE)]).astype(BF16)

    def branch_end():
        branch.end()
        allow(r["credit"].at[0])

    def second_norm():
        def rows(part, _):
            values = tok[part].astype(F32) + total[part]
            r["resid"][part] = values
            seq_a[mine(part)] = (values * norm_scale(values) * gains[1:2, :]).astype(BF16)
            return 0

        by_rows(seg, rows)
        pl.semaphore_wait(r["credit"].at[0], 3)

    def hidden(k, start, units, t):
        ref, here = weights[k], block(t)
        gate = dot(seq_a[here], ref[:, pl.ds(0, units)])
        upval = dot(seq_a[here], ref[:, pl.ds(units, units)])
        dact = dot(seq_b[here], ref[:, pl.ds(2 * units, units)])
        sigma = jax.nn.sigmoid(gate)
        silu = gate * sigma
        act[here, pl.ds(start, units)] = (silu * upval).astype(BF16)
        dgate = dact * upval * sigma * (1.0 + gate * (1.0 - sigma))
        du[here, pl.ds(2 * start, units)] = dgate.astype(BF16)
        du[here, pl.ds(2 * start + units, units)] = (dact * silu).astype(BF16)

    def slice_of(n):
        return jnp.where(outer < layers // 2, D // SLICE - 1 - n, n)

    def gate_up_grads(k, start, units, n):
        part = slice_of(n)
        left = seq_a[:, aligned(part * SLICE, SLICE, 128)]
        reduce.grads[k][aligned(part * SLICE, SLICE), pl.ds(0, 2 * units)] = dot_columns(
            left, du[:, pl.ds(2 * start, 2 * units)]
        ).astype(BF16)

    def down_grads(k, start, units, n):
        part = slice_of(n)
        left = seq_b[:, aligned(part * SLICE, SLICE, 128)]
        reduce.grads[k][aligned(part * SLICE, SLICE), pl.ds(2 * units, units)] = dot_columns(
            left, act[:, pl.ds(start, units)]
        ).astype(BF16)

    def grads(k, start, units, n):
        gate_up_grads(k, start, units, n)
        down_grads(k, start, units, n)
        reduce.direct(k, slice_of(n))

    def second(t):
        here = block(t)
        seq_b[here] = sum(
            dot_rows(du[here, pl.ds(2 * start, 2 * units)], weights[k][:, pl.ds(0, 2 * units)])
            for k, start, units in chunks
        ).astype(BF16)

    def down_end():
        down.end()
        reload().start()
        allow(r["credit"].at[1])

    def forward(t):
        here = block(t)
        du[here, pl.ds(0, D)] = sum(
            dot_rows(act[here, pl.ds(start, units)], weights[k][:, pl.ds(2 * units, units)])
            for k, start, units in chunks
        ).astype(BF16)

    def second_back():
        def rows(part, gain):
            dpart, dgain = norm_back(r["resid"][part], gains[1:2, :], total[part])
            dresid = cot[part].astype(F32) + dpart
            r["dresid"][part] = dresid
            seq_a[mine(part)] = dresid.astype(BF16)
            return gain + dgain

        sums[...] = jnp.zeros(sums.shape, F32)
        tap_sums[...] = jnp.zeros(tap_sums.shape, F32)
        sums[1:2, pl.ds(0, D)] = by_rows(seg, rows, jnp.zeros((1, D), F32))
        pl.semaphore_wait(r["credit"].at[1], 3)

    def mix_back(t):
        s, here = t // 2, block(t)
        dmixed = pltpu.roll(dot(seq_a[here], weights[0][:, pl.ds(512, WIDE)]), WIDE - 64, 1)
        dmixed = jnp.where(lanes, dmixed, 0.0)
        for i in (0, 1):

            @pl.when(t % 2 == i)
            def _():
                du[here, kept] = (dmixed * convolved(s, i)).astype(BF16)
                c_all[s, pl.ds(i * seg, seg)] = dmixed * c_all[s, pl.ds(i * seg, seg)]

    def after():
        return remote(
            c_all.at[:, pl.ds(0, 8)], c_all.at[:, pl.ds(2 * seg, 8)], r["halo_send"].at[1], r["halo_recv"].at[1], at(-1)
        )

    def halo_back():
        pl.when(outer > 0)(lambda: after().start())

        @pl.when(outer == layers - 1)
        def _():
            c_all[:, pl.ds(2 * seg, 8)] = jnp.zeros((GROUPS, 8, WIDE), F32)

    def conv_back(n):
        for i in (0, 1):
            pl.when(n // GROUPS == i)(functools.partial(conv_back_half, n % GROUPS, i))

    def conv_back_half(s, i):
        t = block(2 * s + i)
        dconv = c_all[s, pl.ds(i * seg, seg)]
        dgated = (
            taps[2:3, :] * dconv
            + taps[1:2, :] * c_all[s, pl.ds(1 + i * seg, seg)]
            + taps[0:1, :] * c_all[s, pl.ds(2 + i * seg, seg)]
        )
        parts = dot(seq_b[t], weights[0][:, pl.ds(0, 640)])
        db = dgated * parts[:, 384:640]
        dx = dgated * parts[:, :WIDE]
        dc = jnp.concatenate([du[t, kept].astype(F32), jnp.zeros((seg, 128), F32)], axis=1)
        dc = pltpu.roll(dc, 64, 1)
        act[t, pl.ds(0, 128)] = db[:, :128].astype(BF16)
        act[t, pl.ds(128, 128)] = (db[:, 128:] + dc[:, :128]).astype(BF16)
        act[t, pl.ds(256, 128)] = dc[:, 128:256].astype(BF16)
        act[t, pl.ds(384, WIDE)] = dx.astype(BF16)
        act[t, pl.ds(640, 128)] = jnp.zeros((seg, 128), BF16)
        for k in range(3):
            moved = gated[s, pl.ds(6 + k + i * seg, seg)]
            tap_sums[k : k + 1] = tap_sums[k : k + 1] + jnp.sum(dconv * moved, axis=0, keepdims=True)

    def conv_grads(n):
        part = slice_of(n)
        held_rows, cols = aligned(part * SLICE, SLICE), aligned(part * SLICE, SLICE, 128)
        ref = reduce.grads[0]
        of_parts = dot_columns(seq_b[:, cols], act[:, pl.ds(0, CONV_COLS)])
        ref[held_rows, pl.ds(0, 512)] = of_parts[:, :512].astype(BF16)
        of_mixed = dot_columns(seq_a[:, cols], mixed[...])
        ref[held_rows, pl.ds(512, WIDE)] = (of_parts[:, 512:] + of_mixed).astype(BF16)
        reduce.direct(0, part)

    def feed_end():
        feed.end()
        allow(r["credit"].at[2])
        r["block_out"][...] = (r["resid"][...] + total[...]).astype(BF16)

    def first(t):
        here = block(t)
        seq_a[here] = dot_rows(act[here, pl.ds(0, 640)], weights[0][:, pl.ds(0, 640)]).astype(BF16)

    def first_back():
        def rows(part, gain):
            dpart, dgain = norm_back(tok[part].astype(F32), gains[0:1, :], total[part])
            r["input_grad"][part] = (r["dresid"][part] + dpart).astype(BF16)
            return gain + dgain

        sums[0:1, pl.ds(0, D)] = by_rows(seg, rows, jnp.zeros((1, D), F32))
        sums[2:5, aligned(me * WIDE, WIDE, 128)] = tap_sums[0:3]

    def gains_across(n):
        return remote(sums, r["gain_in"].at[n], r["send_a"].at[n], r["recv_a"].at[n], partners()[n])

    def gains_add(n):
        gains_across(n).wait()
        sums[...] = sums[...] + r["gain_in"][n]

    def line_copy(sign, steps):
        slot = (0 if sign > 0 else 1, steps - 1)
        return remote(
            sums, r["gain_line"].at[slot], r["send_l"].at[slot], r["recv_l"].at[slot], at(sign * steps)
        )

    def gains_line():
        for steps in range(1, layers):
            for sign in (1, -1):
                pl.when(in_line(outer + sign * steps, layers))(line_copy(sign, steps).start)

    def gains_end():
        for steps in range(1, layers):
            for sign in (1, -1):
                pl.when(in_line(outer + sign * steps, layers))(line_copy(sign, steps).wait_send)
                pl.when(in_line(outer - sign * steps, layers))(line_copy(sign, steps).wait_recv)

        own_sums = sums[...]
        for origin in range(layers):
            for steps in range(1, layers):
                for sign in (1, -1):

                    @pl.when((outer - sign * steps == origin))
                    def _():
                        came = r["gain_line"][0 if sign > 0 else 1, steps - 1]
                        sums[...] = came if origin == 0 else sums[...] + came

            if origin > 0:

                @pl.when(outer == origin)
                def _():
                    sums[...] = sums[...] + own_sums

    def end():
        reduce.finish(0)
        for k in range(len(WIDTHS)):
            reduce.wait_sent(k)
        pl.when(outer < layers - 1)(lambda: ahead().wait_send())
        pl.when(outer > 0)(lambda: after().wait_send())

    windows = [
        (r["resid"], 0, D), (r["dresid"], D, D), (total, 2 * D, D), (r["resid"], 3 * D, D),
        (r["tail"], 4 * D, GROUP_COLS - 4 * D),
    ]

    def load(n):
        ref, first, width = windows[n]
        return pltpu.make_async_copy(
            r["weights"].at[:, pl.ds(first, width)], ref.at[pl.ds(0, rows)], r["loaded"].at[n]
        )

    def start():
        for n in (0, 1, 2, 4):
            load(n).start()
        greet(layers)
        load(0).wait()
        cut(0)
        load(3).start()
        greeted(layers)

    def cut(k):
        def read(part, first, width):
            found = []
            for n, (ref, low, size) in enumerate(windows):
                start, stop = max(first, low), min(first + width, low + size)
                if start < stop and (n == 0) == (k == 0):
                    found.append(ref[part, start - low : stop - low])
            return found

        size = band(rows, 96)

        def cut_band(n, _):
            part = aligned(n * size, size)
            halves = []
            for half in (0, 1):
                pieces = []
                for first, own, width, padding in column_pieces(half):
                    if STARTS[k] <= own < STARTS[k] + WIDTHS[k]:
                        pieces += read(part, first, width)
                        if padding:
                            pieces.append(jnp.zeros((size, padding), F32))
                halves.append(jnp.concatenate(pieces, axis=1))
            is_low = inner == 0
            seq = lax.axis_index("seq")
            own_rows = aligned(seq * rows + n * size, size)
            weights[k][own_rows, :] = jnp.where(is_low, halves[0], halves[1]).astype(BF16)
            gather.other_rows(k)[part, :] = jnp.where(is_low, halves[1], halves[0]).astype(BF16)
            return 0

        for n in (1, 2, 3, 4) if k == CUT_FIRST else ():
            load(n).wait()
        lax.fori_loop(0, rows // size, cut_band, 0)

    def hold():
        held().start()

    def hold_end():
        held().wait()

    def halo_end():
        pl.when(outer > 0)(lambda: ahead().wait_recv())

    def reload_end():
        reload().wait()

    def halo_back_end():
        pl.when(outer < layers - 1)(lambda: after().wait_recv())

    def feed_credit():
        pl.semaphore_wait(r["credit"].at[2], 3)

    def from_spread(moved, body):
        def step(n):
            for m in range(8):
                if moved.before(m):

                    @pl.when(n == m)
                    def _():
                        for act in moved.before(m):
                            act()

            body(moved.index(n))

        return step

    def each(body, *cases):
        return [functools.partial(body, *(case if isinstance(case, tuple) else (case,))) for case in cases]

    every = range(len(WIDTHS))
    cuts = each(cut, *every)
    exchange, send_own, send_other = (
        each(body, *every) for body in (gather.exchange, gather.send_own, gather.send_other)
    )
    step = [each(gather.steps, (k, 1, 1), (k, 2, 2), (k, 3)) for k in every]
    join_far = each(reduce.join, *((k, layers - 2, 2) for k in every))
    join_near = each(reduce.join, *((k, 1, 1) for k in every))
    final = each(reduce.final, (0, 3), 1, (2, 1), (3, 2))
    feed_pair = each(feed.add_pair, 0, 1, 2)
    gain_send = [lambda n=n: gains_across(n).start() for n in range(3)]
    gain_add = each(gains_add, 0, 1, 2)
    d3_far = functools.partial(reduce.direct, 3, least=2)
    d3_near = functools.partial(reduce.direct, 3, most=1)
    blocks, parts = 2 * GROUPS, D // SLICE
    proj = Loop(GROUPS, project)
    mix = Loop(blocks, lambda n: branch.make(n, convolve))
    hid1 = Loop(blocks, from_spread(two, functools.partial(hidden, *chunks[0])))
    hid2, hid3 = (Loop(blocks, functools.partial(hidden, *chunk)) for chunk in chunks[1:])
    grad1, grad2 = (Loop(parts, functools.partial(grads, *chunk)) for chunk in chunks[:2])
    down3 = Loop(parts, functools.partial(down_grads, *chunks[2]))
    back2 = Loop(blocks, lambda n: down.make(n, second))
    gate3 = Loop(parts, functools.partial(gate_up_grads, *chunks[2]))
    ffn = Loop(blocks, forward)
    back_mix = Loop(blocks, from_spread(three, mix_back))
    back_conv = Loop(blocks, conv_back)
    grad0 = Loop(parts, conv_grads)
    back1 = Loop(blocks, lambda n: inputs.make(n, first))
    play(
        [
            start, send_own[0], exchange[0], cuts[1], first_norm, one.start, exchange[1], send_other[0], step[0][0],
            cuts[3], one.first, cuts[2], step[0][1], up_start, send_own[1], one.near, one.far, step[0][2], one.end,
            hold, proj[0], proj[1], exchange[3], hold_end, proj[2], proj[3], up.first, halo, exchange[2],
            send_other[1], halo_end, mix[0], step[1][0], mix[1], up.near, mix[2], mix[3], mix[4], up.far, up.end,
            mix[5], send_other[2], step[1][1], mix[6], send_own[2], mix[7], branch_end, second_norm, two.start,
            step[1][2], send_own[3], hid1[0], hid1[1], hid1[2], hid1[3], send_other[3], step[2][0], hid1[4],
            hid1[5], hid1[6], hid1[7], two.sent, gather.crossed, grad1[0], grad1[1], step[2][1], grad1[2],
            step[2][2], grad1[3], hid2[0], hid2[1], hid2[2], hid2[3], step[3][0], hid2[4], hid2[5], hid2[6],
            hid2[7], join_far[1], grad2[0], grad2[1], grad2[2], grad2[3], step[3][1], step[3][2], hid3[0], hid3[1],
            hid3[2], hid3[3], hid3[4], hid3[5], hid3[6], hid3[7], down3[0], down3[1], down3[2], down3[3], back2[0],
            back2[1], back2[2], back2[3], back2[4], back2[5], back2[6], back2[7], gate3[0], join_near[1],
            join_far[2], gate3[1], gather.finish, gate3[2], gate3[3], down_end, second_back, three.start, ffn[0],
            ffn[1], ffn[2], ffn[3], ffn[4], ffn[5], ffn[6], ffn[7], back_mix[0], d3_far, back_mix[1], feed.push,
            join_near[2], back_mix[2], back_mix[3], reload_end, feed_pair[0], back_mix[4], feed_pair[1],
            back_mix[5], back_mix[6], feed_pair[2], back_mix[7], three.sent, halo_back, back_conv[0], back_conv[1],
            back_conv[2], d3_near, back_conv[3], feed.pass_on, join_far[3], feed.add_own, final[1], halo_back_end,
            back_conv[4], back_conv[5], back_conv[6], join_near[3], back_conv[7], grad0[0], grad0[1], grad0[2],
            grad0[3], feed_end, feed_credit, back1[0], back1[1], back1[2], back1[3], back1[4], join_far[0],
            back1[5], back1[6], final[2], back1[7], join_near[0], inputs.end, first_back, gain_send[0], final[3],
            gain_add[0], gain_send[1], gain_add[1], gain_send[2], gain_add[2], gains_line, final[0], gains_end, end,
        ]
    )


class Loop:
    def __init__(self, count, body):
        self.count, self.body = count, body

    def __getitem__(self, n):
        return (self, n)


def play(order):
    order = list(order)
    while order:
        entry = order.pop(0)
        if not isinstance(entry, tuple):
            entry()
            continue
        loop, _ = entry
        between = {}
        for n in range(1, loop.count):
            between[n] = []
            while order[0] != (loop, n):
                between[n].append(order.pop(0))
            order.pop(0)

        def turn(n, _):
            for m, acts in between.items():
                if acts:

                    @pl.when(n == m)
                    def _():
                        play(acts)

            loop.body(n)
            return 0

        lax.fori_loop(0, loop.count, turn, 0)


def block_step(tok, cot, gains, weights, layers):
    rows, seg = weights.shape[0], tok.shape[0]
    count = len(WIDTHS)
    tokens = 2 * GROUPS * seg
    vmem, anywhere = pl.BlockSpec(memory_space=pltpu.VMEM), pl.BlockSpec(memory_space=pl.ANY)
    shape, scratch = jax.ShapeDtypeStruct, pltpu.VMEM
    dma, regular = pltpu.SemaphoreType.DMA, pltpu.SemaphoreType.REGULAR
    hops = layers - 1
    wide, biggest = sum(WIDTHS), max(WIDTHS)
    out_shape = [
        shape((seg, D), BF16),
        shape((seg, D), BF16),
        shape((8, 2 * GROUPS * WIDE), F32),
        shape((rows, wide), F32),
        shape((rows, wide), BF16),
        shape((tokens, D), BF16),
    ] + [shape((2, hops, 2 * rows, width), BF16) for width in WIDTHS]
    scratch_shapes = (
        [scratch((D, width), BF16) for width in WIDTHS]
        + [
            scratch((tokens, D), BF16),
            scratch((tokens, D), BF16),
            scratch((tokens, 2 * PAD_F), BF16),
            scratch((tokens, PAD_F), BF16),
            scratch((GROUPS, 8 + 2 * seg, WIDE), F32),
            scratch((GROUPS, 8 + 2 * seg, WIDE), F32),
            scratch((tokens, WIDE), BF16),
            scratch((seg, D), F32),
            scratch((seg, D), F32),
            scratch((seg, D), F32),
            scratch((4, seg, D), BF16),
            scratch((2, seg, D), BF16),
            scratch((seg, D), BF16),
        ]
        + [scratch((D, width), BF16) for width in WIDTHS[1:]]
        + [
            scratch((2 * rows, biggest), BF16),
            scratch((rows, biggest), F32),
            scratch((rows, GROUP_COLS - 4 * D), F32),
            scratch((rows, wide), BF16),
            scratch((8, WIDE), F32),
            scratch((3, 8, 2 * GROUPS * WIDE), F32),
            scratch((2, hops, 8, 2 * GROUPS * WIDE), F32),
            dma,
            dma((5,)),
            dma((count,)),
            dma((count,)),
            dma((count, 2, hops, 2)),
            dma((count, 2, hops, 2)),
            dma((4, 11)),
            dma((4, 11)),
            dma((4, 10)),
            dma((4, 10)),
            regular((3,)),
            dma((2,)),
            dma((2,)),
            dma((count, 2, hops)),
            dma((count, 2, hops)),
            dma,
            dma((4,)),
            dma((count,)),
            dma((count,)),
            dma((count,)),
            dma((3,)),
            dma((3,)),
            dma((2, hops)),
            dma((2, hops)),
        ]
    )
    return pl.pallas_call(
        functools.partial(block_kernel, layers, rows),
        out_shape=out_shape,
        in_specs=[vmem] * 3 + [anywhere],
        out_specs=[vmem] * 3 + [anywhere] * (3 + count),
        scratch_shapes=scratch_shapes,
        compiler_params=pltpu.CompilerParams(
            collective_id=0, has_side_effects=True, vmem_limit_bytes=VMEM_BYTES
        ),
        name="block_step",
    )(tok, cot, gains, weights)[:5]


def band(rows, most):
    return max(size for size in range(16, most + 1, 16) if rows % size == 0)


def adam_update(param, grad, first, second, rate, decay):
    first_new = MOMENT_DECAY * first + (1.0 - MOMENT_DECAY) * grad
    second_new = SQUARE_DECAY * second + (1.0 - SQUARE_DECAY) * grad * grad
    root = jnp.sqrt(second_new * (1.0 / (1.0 - SQUARE_DECAY**STEP))) + ADAM_EPSILON
    step = first_new * (rate / (1.0 - MOMENT_DECAY**STEP)) / root
    return (first_new, second_new, param * (1.0 - rate * decay) - step)


def update_kernel(
    inner_ref, mine_ref, theirs_ref, weights_ref, first_ref, second_ref, sums_ref, gains_ref, gains_first_ref,
    gains_second_ref, block_ref, input_ref, grad_out, first_out, second_out, weights_out, gains_grad_out,
    gains_first_out, gains_second_out, gains_out, block_out, input_out,
):
    is_low = inner_ref[0] == 0
    mine, theirs = mine_ref[...], theirs_ref[...].astype(F32)
    for half in (0, 1):
        chosen = jnp.where(is_low, mine, theirs) if half == 0 else jnp.where(is_low, theirs, mine)
        for first, own, width, _ in column_pieces(half):
            grad_out[:, first : first + width] = chosen[:, own : own + width]
    first_out[...], second_out[...], weights_out[...] = adam_update(
        weights_ref[...], grad_out[...], first_ref[...], second_ref[...], WEIGHT_RATE, WEIGHT_DECAY
    )

    @pl.when(pl.program_id(0) == 0)
    def _():
        gains_grad_out[0:2] = sums_ref[0:2, :D]
        for n in range(2 * GROUPS):
            gains_grad_out[2:5, n * HALF_Q : (n + 1) * HALF_Q] = sums_ref[2:5, n * WIDE : n * WIDE + HALF_Q]
        gains_first_out[...], gains_second_out[...], gains_out[...] = adam_update(
            gains_ref[...], gains_grad_out[...], gains_first_ref[...], gains_second_ref[...], GAIN_RATE, 0.0
        )
        block_out[...] = block_ref[...]
        input_out[...] = input_ref[...]


def update(inner, mine, theirs, weights, first, second, sums, gains, gains_first, gains_second, block, grad):
    rows, cols = weights.shape
    wide = mine.shape[1]
    size = band(rows, 32)
    by_row = lambda width: pl.BlockSpec((size, width), lambda n: (n, 0))
    whole = lambda values: pl.BlockSpec(values.shape, lambda n: (0, 0))
    shape = jax.ShapeDtypeStruct
    return pl.pallas_call(
        update_kernel,
        grid=(rows // size,),
        out_shape=[shape((rows, cols), F32)] * 4 + [shape(gains.shape, F32)] * 4 + [shape(block.shape, BF16)] * 2,
        in_specs=[pl.BlockSpec(memory_space=pltpu.SMEM)]
        + [by_row(wide)] * 2
        + [by_row(cols)] * 3
        + [whole(sums)]
        + [whole(gains)] * 3
        + [whole(block)] * 2,
        out_specs=[by_row(cols)] * 4 + [whole(gains)] * 4 + [whole(block)] * 2,
        compiler_params=pltpu.CompilerParams(vmem_limit_bytes=VMEM_BYTES),
        name="update",
    )(inner, mine, theirs, weights, first, second, sums, gains, gains_first, gains_second, block, grad)


def on_device(
    tokens, gains_taps, weights, cotangent, weight_first, weight_second, gains_first, gains_second
):
    layers = lax.axis_size("seq") // 2
    inner_word = (lax.axis_index("seq") % 2).astype(jnp.int32).reshape(1)
    block_out, input_grad, gain_sums, mine, theirs = block_step(
        tokens[0], cotangent[0], gains_taps, weights, layers
    )
    (
        weight_grad, weight_first_new, weight_second_new, weight_new,
        gains_grad, gains_first_new, gains_second_new, gains_new, block_out, input_grad,
    ) = update(
        inner_word, mine, theirs, weights, weight_first, weight_second,
        gain_sums, gains_taps, gains_first, gains_second, block_out, input_grad,
    )
    return (
        block_out[None],
        input_grad[None],
        weight_grad,
        weight_first_new,
        weight_second_new,
        weight_new,
        gains_grad,
        gains_first_new,
        gains_second_new,
        gains_new,
    )


def solution(mesh):
    tokens, rows, whole = P("shard", "seq", None), P("seq", "shard"), P()
    return jax.shard_map(
        on_device,
        mesh=mesh,
        in_specs=(tokens, whole, rows, tokens, rows, rows, whole, whole),
        out_specs=(tokens, tokens, rows, rows, rows, rows, whole, whole, whole, whole),
        check_vma=False,
    )
```

profile of v0, /device:TPU:0, one launch (start us, length us, event | category | flops | bytes accessed | tf_op | source)
XLA Modules:
  0.0 347.4 jit_solution(7168158764634931436)
XLA Ops:
  0.7 329.5 %block_step.1 = (bf16[240,1536]{1,0:T(8,128)(2,1)}, bf16[240,1536]{1,0:T(8,128)(2,1)}, f32[8,2048]{1,0:T(8,128)}, f32[192,3456]{1,0:T(8,128)}, bf16[192,3456]{1,...) custom-call(bf16[240,1536]{1,0:T(8,128)(2,1)} %bitcast.5, ...), custom_call_target="tpu_custom_call" | custom-call | tf_op jit(solution)/shard_map/block_step/pallas_call | solution.py:1177
  330.1 17.1 %update.1 = (f32[192,6720]{1,0:T(8,128)}, f32[192,6720]{1,0:T(8,128)}, f32[192,6720]{1,0:T(8,128)}, f32[192,6720]{1,0:T(8,128)}, f32[5,1536]{1,0:T(8,128)}, /*in...) custom-call(s32[1]{0:T(128)} %bitcast.inner_ref, ...), custom_call_target="tpu_custom_call" | custom-call | tf_op jit(solution)/shard_map/update/pallas_call | solution.py:1236
where the time goes:
time: 350 us; the launch traced here: 347 us
  Pallas kernels  347 us (99%)
    pallas_call x1, Pallas kernels, block_step(): pl.pallas_call(functools.partial(block_kernel, layers, rows), out_shape=o...  329 us
    pallas_call x1, Pallas kernels, update(): pl.pallas_call(update_kernel, grid=(rows // size,), out_shape=[shape((row...  17.1 us

commit v1 on v0

--- a/solution.py
+++ b/solution.py
@@ -24,8 +24,8 @@
 UNIT_STARTS = (0, 384, 640)
 WIDTHS = (CONV_COLS,) + tuple(3 * units for units in UNIT_CHUNKS)
 STARTS = tuple(sum(WIDTHS[:k]) for k in range(len(WIDTHS)))
-SPREAD_SPLITS = (208, 208, 64, 128)
-COLLECT_SPLITS = (128, 128, 112, 112)
+SPREAD_SPLITS = (208, 160, 112, 112)
+COLLECT_SPLITS = (128, 128, 96, 112)
 REACH = (1, 1, 1, 1)
 CUT_FIRST = 1
 SLICE = 384
@@ -1044,26 +1044,26 @@
     back1 = Loop(blocks, lambda n: inputs.make(n, first))
     play(
         [
-            start, send_own[0], exchange[0], cuts[1], first_norm, one.start, exchange[1], send_other[0], step[0][0],
-            cuts[3], one.first, cuts[2], step[0][1], up_start, send_own[1], one.near, one.far, step[0][2], one.end,
-            hold, proj[0], proj[1], exchange[3], hold_end, proj[2], proj[3], up.first, halo, exchange[2],
-            send_other[1], halo_end, mix[0], step[1][0], mix[1], up.near, mix[2], mix[3], mix[4], up.far, up.end,
-            mix[5], send_other[2], step[1][1], mix[6], send_own[2], mix[7], branch_end, second_norm, two.start,
-            step[1][2], send_own[3], hid1[0], hid1[1], hid1[2], hid1[3], send_other[3], step[2][0], hid1[4],
-            hid1[5], hid1[6], hid1[7], two.sent, gather.crossed, grad1[0], grad1[1], step[2][1], grad1[2],
-            step[2][2], grad1[3], hid2[0], hid2[1], hid2[2], hid2[3], step[3][0], hid2[4], hid2[5], hid2[6],
-            hid2[7], join_far[1], grad2[0], grad2[1], grad2[2], grad2[3], step[3][1], step[3][2], hid3[0], hid3[1],
-            hid3[2], hid3[3], hid3[4], hid3[5], hid3[6], hid3[7], down3[0], down3[1], down3[2], down3[3], back2[0],
-            back2[1], back2[2], back2[3], back2[4], back2[5], back2[6], back2[7], gate3[0], join_near[1],
-            join_far[2], gate3[1], gather.finish, gate3[2], gate3[3], down_end, second_back, three.start, ffn[0],
-            ffn[1], ffn[2], ffn[3], ffn[4], ffn[5], ffn[6], ffn[7], back_mix[0], d3_far, back_mix[1], feed.push,
-            join_near[2], back_mix[2], back_mix[3], reload_end, feed_pair[0], back_mix[4], feed_pair[1],
-            back_mix[5], back_mix[6], feed_pair[2], back_mix[7], three.sent, halo_back, back_conv[0], back_conv[1],
-            back_conv[2], d3_near, back_conv[3], feed.pass_on, join_far[3], feed.add_own, final[1], halo_back_end,
-            back_conv[4], back_conv[5], back_conv[6], join_near[3], back_conv[7], grad0[0], grad0[1], grad0[2],
-            grad0[3], feed_end, feed_credit, back1[0], back1[1], back1[2], back1[3], back1[4], join_far[0],
-            back1[5], back1[6], final[2], back1[7], join_near[0], inputs.end, first_back, gain_send[0], final[3],
-            gain_add[0], gain_send[1], gain_add[1], gain_send[2], gain_add[2], gains_line, final[0], gains_end, end,
+            start, exchange[0], send_own[0], first_norm, cuts[1], send_other[0], one.start, send_own[1], cuts[2],
+            exchange[1], step[0][0], one.first, up_start, one.near, exchange[2], step[0][1], cuts[3], send_other[1],
+            one.far, step[0][2], one.end, proj[0], proj[1], up.first, up.near, hold, proj[2], proj[3], halo,
+            step[1][0], hold_end, halo_end, mix[0], mix[1], mix[2], mix[3], mix[4], up.far, mix[5], mix[6], mix[7],
+            step[1][1], up.end, exchange[3], send_own[3], send_other[2], send_own[2], branch_end, second_norm,
+            two.start, step[1][2], send_other[3], hid1[0], hid1[1], hid1[2], hid1[3], hid1[4], step[2][0], hid1[5],
+            gather.crossed, hid1[6], hid1[7], two.sent, grad1[0], grad1[1], grad1[2], step[2][1], step[3][0],
+            step[2][2], grad1[3], hid2[0], hid2[1], hid2[2], hid2[3], hid2[4], hid2[5], hid2[6], hid2[7], grad2[0],
+            grad2[1], grad2[2], grad2[3], step[3][1], step[3][2], hid3[0], hid3[1], hid3[2], hid3[3], hid3[4],
+            hid3[5], hid3[6], hid3[7], down3[0], down3[1], down3[2], down3[3], back2[0], back2[1], join_far[1],
+            back2[2], back2[3], back2[4], back2[5], back2[6], back2[7], gate3[0], gate3[1], join_near[1], gate3[2],
+            gate3[3], down_end, second_back, three.start, d3_far, ffn[0], ffn[1], ffn[2], ffn[3], ffn[4], ffn[5],
+            ffn[6], ffn[7], back_mix[0], back_mix[1], feed.push, back_mix[2], join_far[2], feed_pair[0],
+            back_mix[3], gather.finish, back_mix[4], feed_pair[1], back_mix[5], reload_end, back_mix[6],
+            feed_pair[2], back_mix[7], three.sent, halo_back, back_conv[0], join_near[2], back_conv[1], d3_near,
+            back_conv[2], back_conv[3], feed.pass_on, final[1], feed.add_own, halo_back_end, back_conv[4],
+            join_far[3], back_conv[5], back_conv[6], back_conv[7], grad0[0], grad0[1], grad0[2], grad0[3], feed_end,
+            join_near[3], feed_credit, back1[0], back1[1], back1[2], back1[3], back1[4], join_far[0], back1[5],
+            back1[6], final[2], back1[7], join_near[0], inputs.end, first_back, gain_send[0], final[3], gain_add[0],
+            gain_send[1], gain_add[1], gain_send[2], gain_add[2], gains_line, final[0], gains_end, end,
         ]
     )
 

time: 350 us -> 347 us (level)
  no operation moved by 1% of the time
where the time goes in v1:
time: 347 us; the launch traced here: 346 us
  Pallas kernels  346 us (100%)
    pallas_call x1, Pallas kernels, block_step(): pl.pallas_call(functools.partial(block_kernel, layers, rows), out_shape=o...  328 us
    pallas_call x1, Pallas kernels, update(): pl.pallas_call(update_kernel, grid=(rows // size,), out_shape=[shape((row...  17.1 us

profile of v1, /device:TPU:0, one launch (start us, length us, event | category | flops | bytes accessed | tf_op | source)
XLA Modules:
  0.0 346.4 jit_solution(3631818877337897945)
XLA Ops:
  0.7 328.5 %block_step.1 = (bf16[240,1536]{1,0:T(8,128)(2,1)}, bf16[240,1536]{1,0:T(8,128)(2,1)}, f32[8,2048]{1,0:T(8,128)}, f32[192,3456]{1,0:T(8,128)}, bf16[192,3456]{1,...) custom-call(bf16[240,1536]{1,0:T(8,128)(2,1)} %bitcast.5, ...), custom_call_target="tpu_custom_call" | custom-call | tf_op jit(solution)/shard_map/block_step/pallas_call | solution.py:1177
  329.1 17.1 %update.1 = (f32[192,6720]{1,0:T(8,128)}, f32[192,6720]{1,0:T(8,128)}, f32[192,6720]{1,0:T(8,128)}, f32[192,6720]{1,0:T(8,128)}, f32[5,1536]{1,0:T(8,128)}, /*in...) custom-call(s32[1]{0:T(128)} %bitcast.inner_ref, ...), custom_call_target="tpu_custom_call" | custom-call | tf_op jit(solution)/shard_map/update/pallas_call | solution.py:1236
